TPU v7x, 32 devices: a whole 2x2x4 slice. The times are simulated.
32 devices in a mesh: groups: 2 (over x), cuts: 16 (over z, y, core).
Axes of the slice: x: 2, y: 2, z: 4, core: 2. Of those that a mesh axis runs over, the one named last changes fastest.
Arguments:
- displacement: float32 [2, 5, 5, 5, 32, 256], P(None, None, None, None, ('groups', 'cuts')), parts along dimension 4, may hold values from -6 to 6
- velocity: float32 [2, 5, 5, 5, 32, 256], P(None, None, None, None, ('groups', 'cuts')), parts along dimension 4, may hold values from -6 to 6
- modulus: float32 [32, 256], P(('groups', 'cuts')), parts along dimension 0, may hold values from 0.5 to 2
- density: float32 [32, 256], P(('groups', 'cuts')), parts along dimension 0, may hold values from 0.5 to 2
- adjoint_source: float32 [5, 5, 5, 32, 256], P(None, None, None, ('groups', 'cuts')), parts along dimension 3, may hold values from -6 to 6
- database: float32 [16384, 100], P(('groups', 'cuts')), parts along dimension 0, may hold values from -24 to 24
- face_source: int32 [2048, 1], P(('groups', 'cuts')), parts along dimension 0, may hold values from 0 to 15; in each aligned block of 64 rows (0 to 63, 64 to 127, ...) at most 16 rows name the same one
- face_slot: int32 [2048], P(('groups', 'cuts')), parts along dimension 0, may hold values from 0 to 511
Outputs:
- new_displacement: float32 [2, 5, 5, 5, 32, 256], P(None, None, None, None, ('groups', 'cuts')), parts along dimension 4
- new_velocity: float32 [2, 5, 5, 5, 32, 256], P(None, None, None, None, ('groups', 'cuts')), parts along dimension 4
- kernel: float32 [5, 5, 5, 32, 256], P(None, None, None, ('groups', 'cuts')), parts along dimension 3
There are 2 independent parts, one for each index of `groups`. A program takes and returns all parts, laid end to end along the dimension named above; each array names one. Nothing has to cross between parts.
Inputs may be any that keep to these rules, and one draw needn't show every extreme that they name: `face_source`: no more than 16 faces of one slab name the same source, a bound that some block reaches.
All inputs are finite; a program needn't handle non-finite values.
Results may differ from a plain program's by a relative error of at most 0.0001.
Values sent between devices are 32-bit elements; how exact they have to be, the bound alone decides.
A program may use at most 64 MiB of HBM per device.

v0:
```python
import functools
import math

import jax
import jax.numpy as jnp
import numpy as np
from jax import lax
from jax.experimental import pallas as pl
from jax.experimental.pallas import tpu as pltpu
from jax.sharding import PartitionSpec as P

EDGE = 16
STEPS = 4
TIME_STEP = 0.03
MESH = pl.DeviceIdType.MESH


def gll_tables():
    points = np.array([-1.0, -math.sqrt(3.0 / 7.0), 0.0, math.sqrt(3.0 / 7.0), 1.0])
    weights = np.array([0.1, 49.0 / 90.0, 32.0 / 45.0, 49.0 / 90.0, 0.1])
    derivative = np.zeros((5, 5))
    for node_row in range(5):
        for node_col in range(5):
            summed = 0.0
            for other_node in range(5):
                if other_node == node_col:
                    continue
                term = 1.0 / (points[node_col] - points[other_node])
                for third_node in range(5):
                    if third_node != node_col and third_node != other_node:
                        term = (
                            term
                            * (points[node_row] - points[third_node])
                            / (points[node_col] - points[third_node])
                        )
                summed = summed + term
            derivative[node_row, node_col] = summed
    return (derivative, weights)


DERIV, WEIGHTS = gll_tables()
STIFF = DERIV.T @ np.diag(WEIGHTS) @ DERIV
STIFF_W = STIFF / WEIGHTS[:, None]


def mix(row, parts):
    total = None
    for coefficient, part in zip(row, parts):
        if abs(coefficient) < 1e-12:
            continue
        term = float(coefficient) * part
        total = term if total is None else total + term
    return total


def iota(shape, dim):
    return lax.broadcasted_iota(jnp.int32, shape, dim)


def join_plane(plane):
    lane = iota((8, 128), 1)
    half = iota((8, 128), 0) % 2
    column = lane % EDGE
    first, last = plane[:, 0], plane[:, 4]
    from_left = jnp.where(column != 0, pltpu.roll(last, 1, 2), 0.0)
    from_right = jnp.where(column != EDGE - 1, pltpu.roll(first, 127, 2), 0.0)
    plane = jnp.concatenate(
        [(first + from_left)[:, None], plane[:, 1:4], (last + from_right)[:, None]], axis=1
    )
    first, last = plane[0], plane[4]
    rolled = pltpu.roll(last, EDGE, 2)
    under = jnp.where(half != 0, pltpu.roll(rolled, 1, 1), 0.0)
    from_left = jnp.where(lane < EDGE, under, rolled)
    rolled = pltpu.roll(first, 128 - EDGE, 2)
    over = jnp.where(half == 0, pltpu.roll(rolled, 7, 1), 0.0)
    from_right = jnp.where(lane >= 128 - EDGE, over, rolled)
    return jnp.concatenate(
        [(first + from_left)[None], plane[1:4], (last + from_right)[None]], axis=0
    )


def weighted(values):
    rows = [
        jnp.stack([float(WEIGHTS[b] * WEIGHTS[c]) * values for c in range(5)]) for b in range(5)
    ]
    return jnp.stack(rows)


def split(values):
    high = values.astype(jnp.bfloat16)
    low = (values - high.astype(jnp.float32)).astype(jnp.bfloat16)
    return high, low


def dot(left, right):
    return jnp.dot(left, right, preferred_element_type=jnp.float32)


def body_kernel(
    cuts,
    room,
    u_ref,
    v_ref,
    mod_ref,
    den_ref,
    adj_ref,
    db_ref,
    src_ref,
    slot_ref,
    u_out,
    v_out,
    k_out,
    disp,
    vel,
    inv,
    adj,
    ker,
    wmod,
    acc,
    records,
    req,
    req_in,
    rep,
    rep_in,
    den_in,
    face_out,
    face_in,
    req_send,
    req_recv,
    rep_send,
    rep_recv,
    den_send,
    den_recv,
    face_send,
    face_recv,
):
    group = lax.axis_index("groups")
    me = lax.axis_index("cuts")
    has_below = me > 0
    has_above = me < cuts - 1
    below = jnp.maximum(me - 1, 0)
    above = jnp.minimum(me + 1, cuts - 1)
    faces = src_ref.shape[0]
    table = db_ref.shape[0]

    barrier = pltpu.get_barrier_semaphore()

    def greet(k, carry):
        pl.semaphore_signal(
            barrier, inc=1, device_id=(group, lax.rem(me + k, cuts)), device_id_type=MESH
        )
        return carry

    lax.fori_loop(1, cuts, greet, 0)

    target_col = src_ref[...]
    slot_row = slot_ref[...]
    eye = iota((faces, faces), 0) == iota((faces, faces), 1)
    target_row = jnp.sum(jnp.where(eye, target_col, 0), axis=0, keepdims=True)
    same = target_col == target_row
    row_id, col_id = iota((faces, faces), 0), iota((faces, faces), 1)
    rank_row = jnp.sum(jnp.where(same & (row_id < col_id), 1, 0), axis=0, keepdims=True)
    rank_col = jnp.sum(jnp.where(same & (col_id < row_id), 1, 0), axis=1, keepdims=True)
    place_row = target_row * room + rank_row
    place_col = target_col * room + rank_col
    wanted = jnp.where(iota((cuts * room, faces), 0) == place_row, slot_row, 0)
    wanted = jnp.sum(wanted, axis=1, keepdims=True)
    req[...] = jnp.broadcast_to(wanted, (cuts * room, 128)).reshape(cuts, room, 128)

    @pl.when(jnp.logical_not(has_below))
    def _():
        face_in[:, 0] = jnp.zeros((STEPS, 25, 4, 128), jnp.float32)
        den_in[0] = jnp.zeros((2, 128), jnp.float32)

    @pl.when(jnp.logical_not(has_above))
    def _():
        face_in[:, 1] = jnp.zeros((STEPS, 25, 4, 128), jnp.float32)
        den_in[1] = jnp.zeros((2, 128), jnp.float32)

    pl.semaphore_wait(barrier, cuts - 1)

    def req_copy(k):
        peer = lax.rem(me + k, cuts)
        return pltpu.make_async_remote_copy(
            src_ref=req.at[peer],
            dst_ref=req_in.at[me],
            send_sem=req_send.at[k],
            recv_sem=req_recv.at[k],
            device_id=(group, peer),
            device_id_type=MESH,
        )

    def rep_copy(k):
        peer = lax.rem(me + k, cuts)
        return pltpu.make_async_remote_copy(
            src_ref=rep.at[peer],
            dst_ref=rep_in.at[me],
            send_sem=rep_send.at[k],
            recv_sem=rep_recv.at[k],
            device_id=(group, peer),
            device_id_type=MESH,
        )

    def den_copy(up):
        return pltpu.make_async_remote_copy(
            src_ref=den_ref,
            dst_ref=den_in.at[1 - up],
            send_sem=den_send.at[up],
            recv_sem=den_recv.at[up],
            device_id=(group, above if up else below),
            device_id_type=MESH,
        )

    def face_copy(step, up):
        return pltpu.make_async_remote_copy(
            src_ref=face_out.at[step, up],
            dst_ref=face_in.at[step, 1 - up],
            send_sem=face_send.at[step, up],
            recv_sem=face_recv.at[step, up],
            device_id=(group, above if up else below),
            device_id_type=MESH,
        )

    def start_all(make):
        def go(k, carry):
            make(k).start()
            return carry

        lax.fori_loop(1, cuts, go, 0)

    def wait_all(make):
        def go(k, carry):
            copy = make(k)
            copy.wait_send()
            copy.wait_recv()
            return carry

        lax.fori_loop(1, cuts, go, 0)

    start_all(req_copy)

    @pl.when(has_above)
    def _():
        den_copy(1).start()

    @pl.when(has_below)
    def _():
        den_copy(0).start()

    req_in[pl.ds(me, 1)] = req[pl.ds(me, 1)]

    blank = jnp.zeros((125, 8, 128), jnp.float32)
    disp[...] = blank
    vel[...] = blank
    adj[...] = blank
    ker[...] = blank
    disp[:, 0:2, :] = u_ref[0]
    disp[:, 2:4, :] = u_ref[1]
    vel[:, 0:2, :] = v_ref[0]
    vel[:, 2:4, :] = v_ref[1]
    adj[:, 2:4, :] = adj_ref[...]
    modulus = jnp.concatenate([mod_ref[...]] * 4, axis=0)
    density = jnp.concatenate([den_ref[...]] * 4, axis=0)
    wmod[...] = weighted(modulus).reshape(25, 8, 128)
    records[...] = jnp.zeros_like(records)
    high, low = split(db_ref[...])

    wait_all(req_copy)
    asked = req_in[...].reshape(cuts * room, 128)
    pick = jnp.concatenate(
        [
            jnp.where(asked == iota(asked.shape, 1) + at, 1.0, 0.0).astype(jnp.bfloat16)
            for at in range(0, table, 128)
        ],
        axis=1,
    )
    served = dot(pick, high) + dot(pick, low)
    rep[...] = jnp.zeros_like(rep)
    rep[:, :, 0 : served.shape[1]] = served.reshape(cuts, room, served.shape[1])
    start_all(rep_copy)
    rep_in[pl.ds(me, 1)] = rep[pl.ds(me, 1)]

    @pl.when(has_above)
    def _():
        den_copy(1).wait_send()

    @pl.when(has_below)
    def _():
        den_copy(0).wait_send()

    @pl.when(has_below)
    def _():
        den_copy(1).wait_recv()

    @pl.when(has_above)
    def _():
        den_copy(0).wait_recv()

    for a in range(5):
        if a in (0, 1, 4):
            near = density
            if a != 1:
                near = near + jnp.concatenate([den_in[a // 4]] * 4, axis=0)
            mass = join_plane(weighted(near)).reshape(25, 8, 128)
            base = TIME_STEP / mass
        inv[25 * a : 25 * a + 25] = float(1.0 / WEIGHTS[a]) * base

    node = iota((128, 1), 0) % 25

    def weight_of(index):
        return jnp.where(
            (index == 0) | (index == 4),
            float(WEIGHTS[0]),
            jnp.where(index == 2, float(WEIGHTS[2]), float(WEIGHTS[1])),
        )

    face_weight = weight_of(node // 5) * weight_of(node % 5)
    element = iota((faces, EDGE * EDGE), 1)
    face_id = iota((faces, EDGE * EDGE), 0)
    line, column = element // EDGE, element % EDGE
    spots = (
        (column == 0, line),
        (column == EDGE - 1, line),
        (line == 0, column),
        (line == EDGE - 1, column),
    )
    wait_all(rep_copy)
    got = jnp.transpose(rep_in[...].reshape(cuts * room, 128)) * face_weight
    got_high, got_low = split(got)
    for side, (here, along) in enumerate(spots):
        chosen = here & (face_id == along + side * EDGE)
        place = jnp.sum(jnp.where(chosen, place_col + 1, 0), axis=0, keepdims=True) - 1
        put = jnp.where(iota((cuts * room, EDGE * EDGE), 0) == place, 1.0, 0.0)
        put = put.astype(jnp.bfloat16)
        moved = dot(got_high, put) + dot(got_low, put)
        records[side, :, 0, :] = moved[:, 0:128]
        records[side, :, 1, :] = moved[:, 128:256]

    def plane_of(ref, a):
        return ref[25 * a : 25 * a + 25].reshape(5, 5, 8, 128)

    def residual(step, a):
        plane = plane_of(disp, a)
        total = mix(STIFF[a], [plane_of(disp, k) for k in range(5)])
        coupling = STIFF_W * WEIGHTS[a]
        total = total + jnp.stack([mix(coupling[b], [plane[k] for k in range(5)]) for b in range(5)])
        total = total + jnp.stack(
            [mix(coupling[c], [plane[:, k] for k in range(5)]) for c in range(5)], axis=1
        )
        force = plane_of(adj, a) - wmod[...].reshape(5, 5, 8, 128) * total
        at = pl.ds(25 * step + 5 * a, 5)
        force = jnp.concatenate(
            [
                (force[:, 0] + records[0, at])[:, None],
                force[:, 1:4],
                (force[:, 4] + records[1, at])[:, None],
            ],
            axis=1,
        )
        force = jnp.concatenate(
            [
                (force[0] + records[2, at])[None],
                force[1:4],
                (force[4] + records[3, at])[None],
            ],
            axis=0,
        )
        return join_plane(force).reshape(25, 8, 128)

    def advance(a, force):
        rows = slice(25 * a, 25 * a + 25)
        speed = vel[rows] + inv[rows] * force
        vel[rows] = speed
        disp[rows] = disp[rows] + TIME_STEP * speed

    def sensitivity(a):
        plane = plane_of(disp, a)
        total = 0.0
        for grad in (
            mix(DERIV[a], [plane_of(disp, k) for k in range(5)]),
            jnp.stack([mix(DERIV[b], [plane[k] for k in range(5)]) for b in range(5)]),
            jnp.stack([mix(DERIV[c], [plane[:, k] for k in range(5)]) for c in range(5)], axis=1),
        ):
            grad = grad.reshape(25, 8, 128)
            total = total + grad * pltpu.roll(grad, 6, 1)
        rows = slice(25 * a, 25 * a + 25)
        ker[rows] = ker[rows] + total

    def one_step(step, carry):
        for a in (4, 0):
            force = residual(step, a)
            acc[25 * a : 25 * a + 25] = force
            face_out[step, a // 4] = force[:, 0:4]
            if a:

                @pl.when(has_above)
                def _():
                    face_copy(step, 1).start()
            else:

                @pl.when(has_below)
                def _():
                    face_copy(step, 0).start()

        for a in (1, 2, 3):
            acc[25 * a : 25 * a + 25] = residual(step, a)
        for a in range(5):
            sensitivity(a)
        for a in (1, 2, 3):
            advance(a, acc[25 * a : 25 * a + 25])

        @pl.when(has_below)
        def _():
            face_copy(step, 1).wait_recv()

        @pl.when(has_above)
        def _():
            face_copy(step, 0).wait_recv()

        for a in (0, 4):
            other = face_in[step, a // 4]
            other = jnp.concatenate([other, jnp.zeros_like(other)], axis=1)
            advance(a, acc[25 * a : 25 * a + 25] + other)

        @pl.when(has_above)
        def _():
            face_copy(step, 1).wait_send()

        @pl.when(has_below)
        def _():
            face_copy(step, 0).wait_send()

        return carry

    lax.fori_loop(0, STEPS, one_step, 0)

    for field in range(2):
        u_out[field] = disp[:, 2 * field : 2 * field + 2, :]
        v_out[field] = vel[:, 2 * field : 2 * field + 2, :]
    k_out[...] = ker[:, 0:2, :] * (-TIME_STEP * mod_ref[...])


def body(
    displacement, velocity, modulus, density, adjoint_source, database, face_source, face_slot
):
    cuts = lax.axis_size("cuts")
    faces = face_source.shape[0]
    capacity = max(2, 4 * faces // cuts)
    room = -(-capacity // 8) * 8
    vmem = pl.BlockSpec(memory_space=pltpu.VMEM)
    f32 = jnp.float32
    dma = pltpu.SemaphoreType.DMA
    big = pltpu.VMEM((125, 8, 128), f32)
    out = pl.pallas_call(
        functools.partial(body_kernel, cuts, room),
        out_shape=(
            jax.ShapeDtypeStruct((2, 125, 2, 128), f32),
            jax.ShapeDtypeStruct((2, 125, 2, 128), f32),
            jax.ShapeDtypeStruct((125, 2, 128), f32),
        ),
        in_specs=[vmem] * 8,
        out_specs=(vmem, vmem, vmem),
        scratch_shapes=[
            big,
            big,
            big,
            big,
            big,
            pltpu.VMEM((25, 8, 128), f32),
            big,
            pltpu.VMEM((4, 128, 8, 128), f32),
            pltpu.VMEM((cuts, room, 128), jnp.int32),
            pltpu.VMEM((cuts, room, 128), jnp.int32),
            pltpu.VMEM((cuts, room, 128), f32),
            pltpu.VMEM((cuts, room, 128), f32),
            pltpu.VMEM((2, 2, 128), f32),
            pltpu.VMEM((STEPS, 2, 25, 4, 128), f32),
            pltpu.VMEM((STEPS, 2, 25, 4, 128), f32),
            dma((cuts,)),
            dma((cuts,)),
            dma((cuts,)),
            dma((cuts,)),
            dma((2,)),
            dma((2,)),
            dma((STEPS, 2)),
            dma((STEPS, 2)),
        ],
        compiler_params=pltpu.CompilerParams(
            collective_id=0, has_side_effects=True, vmem_limit_bytes=40 * 1024 * 1024
        ),
    )(
        displacement.reshape(2, 125, 2, 128),
        velocity.reshape(2, 125, 2, 128),
        modulus.reshape(2, 128),
        density.reshape(2, 128),
        adjoint_source.reshape(125, 2, 128),
        database,
        face_source,
        face_slot.reshape(1, faces),
    )
    return (
        out[0].reshape(displacement.shape),
        out[1].reshape(velocity.shape),
        out[2].reshape(adjoint_source.shape),
    )


def solution(mesh):
    return jax.shard_map(
        body,
        mesh=mesh,
        in_specs=(
            P(None, None, None, None, ("groups", "cuts"), None),
            P(None, None, None, None, ("groups", "cuts"), None),
            P(("groups", "cuts"), None),
            P(("groups", "cuts"), None),
            P(None, None, None, ("groups", "cuts"), None),
            P(("groups", "cuts"), None),
            P(("groups", "cuts"), None),
            P(("groups", "cuts")),
        ),
        out_specs=(
            P(None, None, None, None, ("groups", "cuts"), None),
            P(None, None, None, None, ("groups", "cuts"), None),
            P(None, None, None, ("groups", "cuts"), None),
        ),
        check_vma=False,
    )
```

profile of v0, /device:TPU:7, one launch (start us, length us, event | category | flops | bytes accessed | tf_op | source)
XLA Modules:
  0.0 35.0 jit_solution(11876900035646145438)
XLA Ops:
  0.6 0.0 copy-start.5
  0.6 0.0 copy-start.6
  0.7 0.0 copy-start.3
  0.7 0.0 copy-start.4
  0.7 0.0 copy-start
  0.7 0.0 copy-start.1
  0.7 0.6 %copy-done.6 = s32[64,1]{0,1:T(1,128)S(1)} copy-done((s32[64,1]{0,1:T(1,128)S(1)}, s32[64,1]{0,1:T(1,128)}, u32[]{:S(2)}) %copy-start.6) | copy-done | bytes 280
  1.3 0.1 copy.17.src_ref
  1.4 1.1 %copy.16.db_ref = f32[512,100]{1,0:T(8,128)S(1)} copy(f32[512,100]{0,1:T(8,128)} %param.13) | data formatting | bytes 409600 | tf_op args[5]
  2.5 0.0 copy-done.5
  2.5 0.0 copy-done.3
  2.5 0.0 copy-done.4
  2.5 0.0 copy-done
  2.5 0.0 copy-done.1
  2.5 0.0 copy-start.2
  2.5 0.9 %copy-done.2 = f32[5,5,5,1,256]{4,3,2,1,0:T(1,128)S(1)} copy-done((f32[5,5,5,1,256]{4,3,2,1,0:T(1,128)S(1)}, f32[5,5,5,1,256]{4,3,2,1,0:T(1,128)}, u32[]{:S(2)}) %copy-start.2) | copy-done | bytes 128024
  3.4 29.5 %shard_map.103 = (f32[2,125,2,128]{3,2,1,0:T(2,128)S(1)}, f32[2,125,2,128]{3,2,1,0:T(2,128)S(1)}, f32[125,2,128]{2,1,0:T(2,128)S(1)}) custom-call(f32[2,125,2,128]{3,2,1,0:T(2,128)S(1)} %bitcast.11, f32[2,125,2,128]{3,2,1,0:T(2,128)S(1)} %bitcast.12, f32[2,128]{1,0:T(2,128)S(1)} %bitcast.15, f32[2,128]{1,0:T(2,128)S(1)} %bitcast.16, ...), custom_call_target="tpu_custom_call" | custom-call | tf_op jit(solution)/shard_map/pallas_call | solution.py:454
  33.0 0.7 %copy.30 = f32[2,5,5,5,1,256]{5,4,3,2,1,0:T(1,128)} copy(f32[2,5,5,5,1,256]{5,4,3,2,1,0:T(1,128)S(1)} %bitcast.10) | data formatting | bytes 512000
  33.7 0.7 %copy.31 = f32[2,5,5,5,1,256]{5,4,3,2,1,0:T(1,128)} copy(f32[2,5,5,5,1,256]{5,4,3,2,1,0:T(1,128)S(1)} %bitcast.9) | data formatting | bytes 512000
  34.4 0.7 %copy.32 = f32[5,5,5,1,256]{4,3,2,1,0:T(1,128)} copy(f32[5,5,5,1,256]{4,3,2,1,0:T(1,128)S(1)} %bitcast.13) | data formatting | bytes 256000
Async XLA Ops:
  0.6 1.8 %copy-start.5 = (s32[64]{0:T(128)S(1)}, s32[64]{0:T(128)}, u32[]{:S(2)}) copy-start(s32[64]{0:T(128)} %param.15) | copy-start | bytes 772
  0.6 0.7 %copy-start.6 = (s32[64,1]{0,1:T(1,128)S(1)}, s32[64,1]{0,1:T(1,128)}, u32[]{:S(2)}) copy-start(s32[64,1]{0,1:T(1,128)} %param.14) | copy-start | bytes 772
  0.7 1.8 %copy-start.3 = (f32[1,256]{1,0:T(1,128)S(1)}, f32[1,256]{1,0:T(1,128)}, u32[]{:S(2)}) copy-start(f32[1,256]{1,0:T(1,128)} %param.10) | copy-start | bytes 3076
  0.7 1.8 %copy-start.4 = (f32[1,256]{1,0:T(1,128)S(1)}, f32[1,256]{1,0:T(1,128)}, u32[]{:S(2)}) copy-start(f32[1,256]{1,0:T(1,128)} %param.11) | copy-start | bytes 3076
  0.7 1.8 %copy-start = (f32[2,5,5,5,1,256]{5,4,3,2,1,0:T(1,128)S(1)}, f32[2,5,5,5,1,256]{5,4,3,2,1,0:T(1,128)}, u32[]{:S(2)}) copy-start(f32[2,5,5,5,1,256]{5,4,3,2,1,0:T(1,128)} %param.8) | copy-start | bytes 768004
  0.7 1.8 %copy-start.1 = (f32[2,5,5,5,1,256]{5,4,3,2,1,0:T(1,128)S(1)}, f32[2,5,5,5,1,256]{5,4,3,2,1,0:T(1,128)}, u32[]{:S(2)}) copy-start(f32[2,5,5,5,1,256]{5,4,3,2,1,0:T(1,128)} %param.9) | copy-start | bytes 768004
  2.5 0.9 %copy-start.2 = (f32[5,5,5,1,256]{4,3,2,1,0:T(1,128)S(1)}, f32[5,5,5,1,256]{4,3,2,1,0:T(1,128)}, u32[]{:S(2)}) copy-start(f32[5,5,5,1,256]{4,3,2,1,0:T(1,128)} %param.12) | copy-start | bytes 384004
where the time goes:
time: 35.2 us; the launch traced here: 35 us
  Pallas kernels  29.5 us (84%)
  local copies, waits for them, and re-layouts  4.73 us (13%)
  between operations  0.75 us (2%)
    pallas_call x1, Pallas kernels, body(): pl.pallas_call(functools.partial(body_kernel, cuts, room), out_shape=(jax...  29.5 us
    unnamed x19, local copies, waits for them, and re-layouts  4.73 us

commit v1 on v0

--- a/solution.py
+++ b/solution.py
@@ -96,9 +96,33 @@
     return jnp.dot(left, right, preferred_element_type=jnp.float32)
 
 
+def one_hot(mask):
+    return jnp.where(mask, 1.0, 0.0).astype(jnp.bfloat16)
+
+
+def dot_t(left, right):
+    return lax.dot_general(
+        left, right, (((1,), (1,)), ((), ())), preferred_element_type=jnp.float32
+    )
+
+
 def body_kernel(
     cuts,
     room,
+    u_hbm,
+    v_hbm,
+    mod_hbm,
+    den_hbm,
+    adj_hbm,
+    db_hbm,
+    src_hbm,
+    slot_hbm,
+    u_hbm_out,
+    v_hbm_out,
+    k_hbm_out,
+    u_out,
+    v_out,
+    k_out,
     u_ref,
     v_ref,
     mod_ref,
@@ -107,9 +131,6 @@
     db_ref,
     src_ref,
     slot_ref,
-    u_out,
-    v_out,
-    k_out,
     disp,
     vel,
     inv,
@@ -118,6 +139,8 @@
     wmod,
     acc,
     records,
+    puts,
+    flat,
     req,
     req_in,
     rep,
@@ -125,10 +148,14 @@
     den_in,
     face_out,
     face_in,
+    load_sem,
+    store_sem,
     req_send,
     req_recv,
     rep_send,
     rep_recv,
+    late_send,
+    late_recv,
     den_send,
     den_recv,
     face_send,
@@ -140,8 +167,28 @@
     has_above = me < cuts - 1
     below = jnp.maximum(me - 1, 0)
     above = jnp.minimum(me + 1, cuts - 1)
-    faces = src_ref.shape[0]
-    table = db_ref.shape[0]
+    faces = src_ref.shape[1]
+    table = db_ref.shape[1]
+    quarter = room // 4
+    rows = cuts * quarter
+
+    loads = [
+        pltpu.make_async_copy(source, target, load_sem.at[i])
+        for i, (source, target) in enumerate(
+            (
+                (src_hbm, src_ref),
+                (slot_hbm, slot_ref),
+                (den_hbm, den_ref),
+                (db_hbm, db_ref),
+                (mod_hbm, mod_ref),
+                (u_hbm, u_ref),
+                (adj_hbm, adj_ref),
+                (v_hbm, v_ref),
+            )
+        )
+    ]
+    for load in loads:
+        load.start()
 
     barrier = pltpu.get_barrier_semaphore()
 
@@ -152,20 +199,6 @@
         return carry
 
     lax.fori_loop(1, cuts, greet, 0)
-
-    target_col = src_ref[...]
-    slot_row = slot_ref[...]
-    eye = iota((faces, faces), 0) == iota((faces, faces), 1)
-    target_row = jnp.sum(jnp.where(eye, target_col, 0), axis=0, keepdims=True)
-    same = target_col == target_row
-    row_id, col_id = iota((faces, faces), 0), iota((faces, faces), 1)
-    rank_row = jnp.sum(jnp.where(same & (row_id < col_id), 1, 0), axis=0, keepdims=True)
-    rank_col = jnp.sum(jnp.where(same & (col_id < row_id), 1, 0), axis=1, keepdims=True)
-    place_row = target_row * room + rank_row
-    place_col = target_col * room + rank_col
-    wanted = jnp.where(iota((cuts * room, faces), 0) == place_row, slot_row, 0)
-    wanted = jnp.sum(wanted, axis=1, keepdims=True)
-    req[...] = jnp.broadcast_to(wanted, (cuts * room, 128)).reshape(cuts, room, 128)
 
     @pl.when(jnp.logical_not(has_below))
     def _():
@@ -176,6 +209,24 @@
     def _():
         face_in[:, 1] = jnp.zeros((STEPS, 25, 4, 128), jnp.float32)
         den_in[1] = jnp.zeros((2, 128), jnp.float32)
+
+    loads[0].wait()
+    loads[1].wait()
+    target_row = src_ref[...]
+    slot_row = slot_ref[...].astype(jnp.float32)
+    row_id, col_id = iota((faces, faces), 0), iota((faces, faces), 1)
+    eye = row_id == col_id
+    target_col = jnp.sum(jnp.where(eye, target_row, 0), axis=1, keepdims=True)
+    slot_col = jnp.sum(jnp.where(eye, slot_row, 0.0), axis=1, keepdims=True)
+    same = target_col == target_row
+    rank_col = jnp.sum(jnp.where(same & (col_id < row_id), 1, 0), axis=1, keepdims=True)
+    to_target = one_hot(iota((cuts, faces), 0) == target_row)
+    at_rank = jnp.where(iota((faces, 128), 1) == rank_col, slot_col, 0.0)
+    high, low = split(at_rank)
+    wanted = dot(to_target, high) + dot(to_target, low)
+    for peer in range(cuts):
+        req[peer] = wanted[peer : peer + 1]
+    loads[2].wait()
 
     pl.semaphore_wait(barrier, cuts - 1)
 
@@ -193,10 +244,21 @@
     def rep_copy(k):
         peer = lax.rem(me + k, cuts)
         return pltpu.make_async_remote_copy(
-            src_ref=rep.at[peer],
-            dst_ref=rep_in.at[me],
+            src_ref=rep.at[peer, 0],
+            dst_ref=rep_in.at[me, 0],
             send_sem=rep_send.at[k],
             recv_sem=rep_recv.at[k],
+            device_id=(group, peer),
+            device_id_type=MESH,
+        )
+
+    def late_copy(k):
+        peer = lax.rem(me + k, cuts)
+        return pltpu.make_async_remote_copy(
+            src_ref=rep.at[peer, pl.ds(1, STEPS - 1)],
+            dst_ref=rep_in.at[me, pl.ds(1, STEPS - 1)],
+            send_sem=late_send.at[k],
+            recv_sem=late_recv.at[k],
             device_id=(group, peer),
             device_id_type=MESH,
         )
@@ -228,11 +290,16 @@
 
         lax.fori_loop(1, cuts, go, 0)
 
-    def wait_all(make):
+    def wait_in(make):
         def go(k, carry):
-            copy = make(k)
-            copy.wait_send()
-            copy.wait_recv()
+            make(k).wait_recv()
+            return carry
+
+        lax.fori_loop(1, cuts, go, 0)
+
+    def wait_out(make):
+        def go(k, carry):
+            make(k).wait_send()
             return carry
 
         lax.fori_loop(1, cuts, go, 0)
@@ -249,44 +316,70 @@
 
     req_in[pl.ds(me, 1)] = req[pl.ds(me, 1)]
 
-    blank = jnp.zeros((125, 8, 128), jnp.float32)
-    disp[...] = blank
-    vel[...] = blank
-    adj[...] = blank
-    ker[...] = blank
+    place_col = (rank_col // quarter) * rows + target_col * quarter + rank_col % quarter
+    element = iota((faces, EDGE * EDGE), 1)
+    face_id = iota((faces, EDGE * EDGE), 0)
+    line, column = element // EDGE, element % EDGE
+    spots = (
+        (column == 0, line),
+        (column == EDGE - 1, line),
+        (line == 0, column),
+        (line == EDGE - 1, column),
+    )
+    for side, (here, along) in enumerate(spots):
+        chosen = here & (face_id == along + side * EDGE)
+        place = jnp.sum(jnp.where(chosen, place_col + 1, 0), axis=0, keepdims=True) - 1
+        puts[side] = one_hot(iota((cuts * room, EDGE * EDGE), 0) == place)
+    loads[3].wait()
+    high, low = split(db_ref[...])
+    disp[:, 4:8, :] = jnp.zeros((125, 4, 128), jnp.float32)
+    vel[:, 4:8, :] = jnp.zeros((125, 4, 128), jnp.float32)
+    adj[...] = jnp.zeros((125, 8, 128), jnp.float32)
+    ker[...] = jnp.zeros((125, 8, 128), jnp.float32)
+    records[...] = jnp.zeros_like(records)
+    loads[4].wait()
+    loads[5].wait()
     disp[:, 0:2, :] = u_ref[0]
     disp[:, 2:4, :] = u_ref[1]
+    wmod[...] = weighted(jnp.concatenate([mod_ref[...]] * 4, axis=0)).reshape(25, 8, 128)
+
+    wait_in(req_copy)
+    asking = split(jnp.concatenate([req_in[s] for s in range(cuts)], axis=0))
+    spread = one_hot(iota((rows, cuts), 0) // quarter == iota((rows, cuts), 1))
+    repeated = dot(spread, asking[0]) + dot(spread, asking[1])
+    repeated = jnp.concatenate([repeated] * 4, axis=0)
+    spot = iota(repeated.shape, 0)
+    spot = quarter * (spot // rows) + spot % quarter
+    asked = split(jnp.where(iota(repeated.shape, 1) == spot, repeated, 0.0))
+    ones = jnp.ones((128, 128), jnp.bfloat16)
+    asked = (dot(asked[0], ones) + dot(asked[1], ones) + 0.5).astype(jnp.int32)
+    pick = jnp.concatenate(
+        [one_hot(asked == iota(asked.shape, 1) + at) for at in range(0, table, 128)], axis=1
+    )
+    served = dot_t(pick, high) + dot_t(pick, low)
+    served = jnp.concatenate([served, jnp.zeros((4 * rows, 128 - served.shape[1]), jnp.float32)], axis=1)
+    lane = iota((rows, 128), 1)
+
+    def lay_out(step):
+        packed = None
+        for j in range(4):
+            moved = pltpu.roll(served[j * rows : (j + 1) * rows], (32 * j - 25 * step) % 128, 1)
+            packed = moved if j == 0 else jnp.where(lane < 32 * j, packed, moved)
+        for peer in range(cuts):
+            rep[peer, step] = packed[peer * quarter : (peer + 1) * quarter]
+
+    lay_out(0)
+    start_all(rep_copy)
+    for step in range(1, STEPS):
+        lay_out(step)
+    start_all(late_copy)
+    rep_in[pl.ds(me, 1)] = rep[pl.ds(me, 1)]
+
+    loads[6].wait()
+    loads[7].wait()
     vel[:, 0:2, :] = v_ref[0]
     vel[:, 2:4, :] = v_ref[1]
     adj[:, 2:4, :] = adj_ref[...]
-    modulus = jnp.concatenate([mod_ref[...]] * 4, axis=0)
-    density = jnp.concatenate([den_ref[...]] * 4, axis=0)
-    wmod[...] = weighted(modulus).reshape(25, 8, 128)
-    records[...] = jnp.zeros_like(records)
-    high, low = split(db_ref[...])
-
-    wait_all(req_copy)
-    asked = req_in[...].reshape(cuts * room, 128)
-    pick = jnp.concatenate(
-        [
-            jnp.where(asked == iota(asked.shape, 1) + at, 1.0, 0.0).astype(jnp.bfloat16)
-            for at in range(0, table, 128)
-        ],
-        axis=1,
-    )
-    served = dot(pick, high) + dot(pick, low)
-    rep[...] = jnp.zeros_like(rep)
-    rep[:, :, 0 : served.shape[1]] = served.reshape(cuts, room, served.shape[1])
-    start_all(rep_copy)
-    rep_in[pl.ds(me, 1)] = rep[pl.ds(me, 1)]
-
-    @pl.when(has_above)
-    def _():
-        den_copy(1).wait_send()
-
-    @pl.when(has_below)
-    def _():
-        den_copy(0).wait_send()
 
     @pl.when(has_below)
     def _():
@@ -296,6 +389,7 @@
     def _():
         den_copy(0).wait_recv()
 
+    density = jnp.concatenate([den_ref[...]] * 4, axis=0)
     for a in range(5):
         if a in (0, 1, 4):
             near = density
@@ -305,7 +399,7 @@
             base = TIME_STEP / mass
         inv[25 * a : 25 * a + 25] = float(1.0 / WEIGHTS[a]) * base
 
-    node = iota((128, 1), 0) % 25
+    node = iota((128, 1), 0) % 32
 
     def weight_of(index):
         return jnp.where(
@@ -315,31 +409,33 @@
         )
 
     face_weight = weight_of(node // 5) * weight_of(node % 5)
-    element = iota((faces, EDGE * EDGE), 1)
-    face_id = iota((faces, EDGE * EDGE), 0)
-    line, column = element // EDGE, element % EDGE
-    spots = (
-        (column == 0, line),
-        (column == EDGE - 1, line),
-        (line == 0, column),
-        (line == EDGE - 1, column),
-    )
-    wait_all(rep_copy)
-    got = jnp.transpose(rep_in[...].reshape(cuts * room, 128)) * face_weight
-    got_high, got_low = split(got)
-    for side, (here, along) in enumerate(spots):
-        chosen = here & (face_id == along + side * EDGE)
-        place = jnp.sum(jnp.where(chosen, place_col + 1, 0), axis=0, keepdims=True) - 1
-        put = jnp.where(iota((cuts * room, EDGE * EDGE), 0) == place, 1.0, 0.0)
-        put = put.astype(jnp.bfloat16)
-        moved = dot(got_high, put) + dot(got_low, put)
-        records[side, :, 0, :] = moved[:, 0:128]
-        records[side, :, 1, :] = moved[:, 128:256]
+
+    def place_records(first, last):
+        for step in range(first, last):
+            for s in range(cuts):
+                flat[step, s * quarter : (s + 1) * quarter] = rep_in[s, step]
+        parts = []
+        for j in range(4):
+            part = None
+            for step in range(first, last):
+                moved = pltpu.roll(flat[step], (32 * (step - j)) % 128, 1)
+                part = moved if part is None else jnp.where(lane < 32 * step, part, moved)
+            parts.append(part)
+        got = jnp.transpose(jnp.concatenate(parts, axis=0)) * face_weight
+        got = got[32 * first : 32 * last]
+        count = got.shape[0]
+        got = jnp.concatenate(split(got), axis=0)
+        for side in range(4):
+            moved = dot(got, puts[side])
+            moved = moved[0:count] + moved[count:]
+            at = slice(32 * first, 32 * last)
+            records[side, at, 0, :] = moved[:, 0:128]
+            records[side, at, 1, :] = moved[:, 128:256]
 
     def plane_of(ref, a):
         return ref[25 * a : 25 * a + 25].reshape(5, 5, 8, 128)
 
-    def residual(step, a):
+    def stiff(a):
         plane = plane_of(disp, a)
         total = mix(STIFF[a], [plane_of(disp, k) for k in range(5)])
         coupling = STIFF_W * WEIGHTS[a]
@@ -347,8 +443,10 @@
         total = total + jnp.stack(
             [mix(coupling[c], [plane[:, k] for k in range(5)]) for c in range(5)], axis=1
         )
-        force = plane_of(adj, a) - wmod[...].reshape(5, 5, 8, 128) * total
-        at = pl.ds(25 * step + 5 * a, 5)
+        return plane_of(adj, a) - wmod[...].reshape(5, 5, 8, 128) * total
+
+    def joined(step, a, force):
+        at = pl.ds(32 * step + 5 * a, 5)
         force = jnp.concatenate(
             [
                 (force[:, 0] + records[0, at])[:, None],
@@ -386,9 +484,9 @@
         rows = slice(25 * a, 25 * a + 25)
         ker[rows] = ker[rows] + total
 
-    def one_step(step, carry):
+    def one_step(step, first):
         for a in (4, 0):
-            force = residual(step, a)
+            force = joined(step, a, plane_of(acc, a) if first else stiff(a))
             acc[25 * a : 25 * a + 25] = force
             face_out[step, a // 4] = force[:, 0:4]
             if a:
@@ -403,11 +501,15 @@
                     face_copy(step, 0).start()
 
         for a in (1, 2, 3):
-            acc[25 * a : 25 * a + 25] = residual(step, a)
-        for a in range(5):
-            sensitivity(a)
+            acc[25 * a : 25 * a + 25] = joined(step, a, plane_of(acc, a) if first else stiff(a))
+        if not first:
+            for a in range(5):
+                sensitivity(a)
         for a in (1, 2, 3):
             advance(a, acc[25 * a : 25 * a + 25])
+        if first:
+            wait_in(late_copy)
+            place_records(1, STEPS)
 
         @pl.when(has_below)
         def _():
@@ -430,14 +532,66 @@
         def _():
             face_copy(step, 0).wait_send()
 
+    for a in range(5):
+        acc[25 * a : 25 * a + 25] = stiff(a).reshape(25, 8, 128)
+    for a in range(5):
+        sensitivity(a)
+    wait_in(rep_copy)
+    place_records(0, 1)
+    one_step(0, True)
+
+    def later(step, carry):
+        one_step(step, False)
         return carry
 
-    lax.fori_loop(0, STEPS, one_step, 0)
-
+    lax.fori_loop(1, STEPS, later, 0)
+
+    stores = [
+        pltpu.make_async_copy(source, target, store_sem.at[i])
+        for i, (source, target) in enumerate(
+            ((u_out, u_hbm_out), (v_out, v_hbm_out), (k_out, k_hbm_out))
+        )
+    ]
     for field in range(2):
         u_out[field] = disp[:, 2 * field : 2 * field + 2, :]
+    stores[0].start()
+    for field in range(2):
         v_out[field] = vel[:, 2 * field : 2 * field + 2, :]
+    stores[1].start()
     k_out[...] = ker[:, 0:2, :] * (-TIME_STEP * mod_ref[...])
+    stores[2].start()
+    for make in (req_copy, rep_copy, late_copy):
+        wait_out(make)
+
+    @pl.when(has_above)
+    def _():
+        den_copy(1).wait_send()
+
+    @pl.when(has_below)
+    def _():
+        den_copy(0).wait_send()
+
+    for store in stores:
+        store.wait()
+
+
+def store_kernel(u_in, v_in, k_in, u_out, v_out, k_out, u_held, v_held, k_held, sems):
+    held = (u_held, v_held, k_held)
+    inward = [
+        pltpu.make_async_copy(source, target, sems.at[i])
+        for i, (source, target) in enumerate(zip((u_in, v_in, k_in), held))
+    ]
+    outward = [
+        pltpu.make_async_copy(source, target, sems.at[3 + i])
+        for i, (source, target) in enumerate(zip(held, (u_out, v_out, k_out)))
+    ]
+    for copy in inward:
+        copy.start()
+    for copy, onward in zip(inward, outward):
+        copy.wait()
+        onward.start()
+    for copy in outward:
+        copy.wait()
 
 
 def body(
@@ -446,21 +600,35 @@
     cuts = lax.axis_size("cuts")
     faces = face_source.shape[0]
     capacity = max(2, 4 * faces // cuts)
-    room = -(-capacity // 8) * 8
+    room = -(-capacity // 4) * 4
+    quarter = room // 4
     vmem = pl.BlockSpec(memory_space=pltpu.VMEM)
+    hbm = pl.BlockSpec(memory_space=pl.ANY)
     f32 = jnp.float32
     dma = pltpu.SemaphoreType.DMA
     big = pltpu.VMEM((125, 8, 128), f32)
+    shapes = (
+        jax.ShapeDtypeStruct((2, 125, 2, 128), f32),
+        jax.ShapeDtypeStruct((2, 125, 2, 128), f32),
+        jax.ShapeDtypeStruct((125, 2, 128), f32),
+    )
+    operands = (
+        displacement.reshape(2, 125, 2, 128),
+        velocity.reshape(2, 125, 2, 128),
+        modulus.reshape(2, 128),
+        density.reshape(2, 128),
+        adjoint_source.reshape(125, 2, 128),
+        database.T,
+        face_source.reshape(1, faces),
+        face_slot.reshape(1, faces),
+    )
     out = pl.pallas_call(
         functools.partial(body_kernel, cuts, room),
-        out_shape=(
-            jax.ShapeDtypeStruct((2, 125, 2, 128), f32),
-            jax.ShapeDtypeStruct((2, 125, 2, 128), f32),
-            jax.ShapeDtypeStruct((125, 2, 128), f32),
-        ),
-        in_specs=[vmem] * 8,
-        out_specs=(vmem, vmem, vmem),
-        scratch_shapes=[
+        out_shape=shapes,
+        in_specs=[hbm] * 8,
+        out_specs=(hbm, hbm, hbm),
+        scratch_shapes=[pltpu.VMEM(x.shape, x.dtype) for x in shapes + operands]
+        + [
             big,
             big,
             big,
@@ -469,13 +637,19 @@
             pltpu.VMEM((25, 8, 128), f32),
             big,
             pltpu.VMEM((4, 128, 8, 128), f32),
-            pltpu.VMEM((cuts, room, 128), jnp.int32),
-            pltpu.VMEM((cuts, room, 128), jnp.int32),
-            pltpu.VMEM((cuts, room, 128), f32),
-            pltpu.VMEM((cuts, room, 128), f32),
+            pltpu.VMEM((4, cuts * room, EDGE * EDGE), jnp.bfloat16),
+            pltpu.VMEM((STEPS, cuts * quarter, 128), f32),
+            pltpu.VMEM((cuts, 1, 128), f32),
+            pltpu.VMEM((cuts, 1, 128), f32),
+            pltpu.VMEM((cuts, STEPS, quarter, 128), f32),
+            pltpu.VMEM((cuts, STEPS, quarter, 128), f32),
             pltpu.VMEM((2, 2, 128), f32),
             pltpu.VMEM((STEPS, 2, 25, 4, 128), f32),
             pltpu.VMEM((STEPS, 2, 25, 4, 128), f32),
+            dma((8,)),
+            dma((3,)),
+            dma((cuts,)),
+            dma((cuts,)),
             dma((cuts,)),
             dma((cuts,)),
             dma((cuts,)),
@@ -486,18 +660,17 @@
             dma((STEPS, 2)),
         ],
         compiler_params=pltpu.CompilerParams(
-            collective_id=0, has_side_effects=True, vmem_limit_bytes=40 * 1024 * 1024
+            collective_id=0, has_side_effects=True, vmem_limit_bytes=63 * 1024 * 1024
         ),
-    )(
-        displacement.reshape(2, 125, 2, 128),
-        velocity.reshape(2, 125, 2, 128),
-        modulus.reshape(2, 128),
-        density.reshape(2, 128),
-        adjoint_source.reshape(125, 2, 128),
-        database,
-        face_source,
-        face_slot.reshape(1, faces),
-    )
+    )(*operands)
+    out = pl.pallas_call(
+        store_kernel,
+        out_shape=shapes,
+        in_specs=[hbm] * 3,
+        out_specs=(hbm, hbm, hbm),
+        scratch_shapes=[pltpu.VMEM(x.shape, x.dtype) for x in shapes] + [dma((6,))],
+        compiler_params=pltpu.CompilerParams(vmem_limit_bytes=63 * 1024 * 1024),
+    )(*out)
     return (
         out[0].reshape(displacement.shape),
         out[1].reshape(velocity.shape),

time: 35.2 us -> 31.8 us (0.903)
  local copies, waits for them, and re-layouts: 4.73 us -> 0 us
  Pallas kernels: 29.5 us -> 31 us
    unnamed x19 -> x0, local copies, waits for them, and re-layouts: 4.73 us -> none
    pallas_call x1 -> x2, Pallas kernels: 29.5 us -> 31 us  [the longest x1 29.1 us: body(): pl.pallas_call(functools.partial(body_kernel, cuts, room), out_shape=shap...]
where the time goes in v1:
time: 31.8 us; the launch traced here: 31.6 us
  Pallas kernels  31 us (97%)
  between operations  0.64 us (2%)
    pallas_call x1, Pallas kernels, body(): pl.pallas_call(functools.partial(body_kernel, cuts, room), out_shape=shap...  29.1 us
    pallas_call x1, Pallas kernels, body(): pl.pallas_call(store_kernel, out_shape=shapes, in_specs=[hbm] * 3, out_sp...  1.86 us

profile of v1, /device:TPU:7, one launch (start us, length us, event | category | flops | bytes accessed | tf_op | source)
XLA Modules:
  0.0 31.6 jit_solution(3519550423092531191)
XLA Ops:
  0.6 29.1 %shard_map.103 = (f32[2,125,2,128]{3,2,1,0:T(2,128)}, f32[2,125,2,128]{3,2,1,0:T(2,128)}, f32[125,2,128]{2,1,0:T(2,128)}) custom-call(f32[2,125,2,128]{3,2,1,0:T(2,128)} %bitcast.11, f32[2,125,2,128]{3,2,1,0:T(2,128)} %bitcast.12, f32[2,128]{1,0:T(2,128)} %bitcast.15, f32[2,128]{1,0:T(2,128)} %bitcast.16, f32[125,2,128]{2,1,0:T(2,128)} %bitcast.14, ...), custom_call_target="tpu_custom_call" | custom-call | tf_op jit(solution)/shard_map/pallas_call | solution.py:625
  29.7 1.9 %shard_map.104 = (f32[2,125,2,128]{3,2,1,0:T(2,128)}, f32[2,125,2,128]{3,2,1,0:T(2,128)}, f32[125,2,128]{2,1,0:T(2,128)}) custom-call(f32[2,125,2,128]{3,2,1,0:T(2,128)} %get-tuple-element.9.u_in, f32[2,125,2,128]{3,2,1,0:T(2,128)} %get-tuple-element.10.v_in, f32[125,2,128]{2,1,0:T(2,128)} %get-tuple-element.11.k_in), custom_call_target="tpu_custom_call" | custom-call | tf_op jit(solution)/shard_map/pallas_call | solution.py:666

commit v2 on v1

--- a/solution.py
+++ b/solution.py
@@ -484,7 +484,27 @@
         rows = slice(25 * a, 25 * a + 25)
         ker[rows] = ker[rows] + total
 
-    def one_step(step, first):
+    stores = []
+
+    def store(source, target):
+        copy = pltpu.make_async_copy(source, target, store_sem.at[len(stores)])
+        copy.start()
+        stores.append(copy)
+
+    def give(low_row, high_row):
+        rows = slice(low_row, high_row)
+        at = pl.ds(low_row, high_row - low_row)
+        for field in range(2):
+            u_out[field, rows] = disp[rows, 2 * field : 2 * field + 2, :]
+            store(u_out.at[field, at], u_hbm_out.at[field, at])
+            v_out[field, rows] = vel[rows, 2 * field : 2 * field + 2, :]
+            store(v_out.at[field, at], v_hbm_out.at[field, at])
+
+    def give_kernel():
+        k_out[...] = ker[:, 0:2, :] * (-TIME_STEP * mod_ref[...])
+        store(k_out, k_hbm_out)
+
+    def one_step(step, first, last):
         for a in (4, 0):
             force = joined(step, a, plane_of(acc, a) if first else stiff(a))
             acc[25 * a : 25 * a + 25] = force
@@ -510,6 +530,9 @@
         if first:
             wait_in(late_copy)
             place_records(1, STEPS)
+        if last:
+            give_kernel()
+            give(25, 100)
 
         @pl.when(has_below)
         def _():
@@ -523,14 +546,6 @@
             other = face_in[step, a // 4]
             other = jnp.concatenate([other, jnp.zeros_like(other)], axis=1)
             advance(a, acc[25 * a : 25 * a + 25] + other)
-
-        @pl.when(has_above)
-        def _():
-            face_copy(step, 1).wait_send()
-
-        @pl.when(has_below)
-        def _():
-            face_copy(step, 0).wait_send()
 
     for a in range(5):
         acc[25 * a : 25 * a + 25] = stiff(a).reshape(25, 8, 128)
@@ -538,28 +553,29 @@
         sensitivity(a)
     wait_in(rep_copy)
     place_records(0, 1)
-    one_step(0, True)
+    one_step(0, True, False)
 
     def later(step, carry):
-        one_step(step, False)
+        one_step(step, False, False)
         return carry
 
-    lax.fori_loop(1, STEPS, later, 0)
-
-    stores = [
-        pltpu.make_async_copy(source, target, store_sem.at[i])
-        for i, (source, target) in enumerate(
-            ((u_out, u_hbm_out), (v_out, v_hbm_out), (k_out, k_hbm_out))
-        )
-    ]
-    for field in range(2):
-        u_out[field] = disp[:, 2 * field : 2 * field + 2, :]
-    stores[0].start()
-    for field in range(2):
-        v_out[field] = vel[:, 2 * field : 2 * field + 2, :]
-    stores[1].start()
-    k_out[...] = ker[:, 0:2, :] * (-TIME_STEP * mod_ref[...])
-    stores[2].start()
+    lax.fori_loop(1, STEPS - 1, later, 0)
+    one_step(STEPS - 1, False, True)
+    give(0, 25)
+    give(100, 125)
+
+    def sent(k, carry):
+        @pl.when(has_above)
+        def _():
+            face_copy(k, 1).wait_send()
+
+        @pl.when(has_below)
+        def _():
+            face_copy(k, 0).wait_send()
+
+        return carry
+
+    lax.fori_loop(0, STEPS, sent, 0)
     for make in (req_copy, rep_copy, late_copy):
         wait_out(make)
 
@@ -571,19 +587,27 @@
     def _():
         den_copy(0).wait_send()
 
-    for store in stores:
-        store.wait()
+    for copy in stores:
+        copy.wait()
 
 
 def store_kernel(u_in, v_in, k_in, u_out, v_out, k_out, u_held, v_held, k_held, sems):
-    held = (u_held, v_held, k_held)
+    pieces = [
+        (lambda ref, field=field, at=at: ref.at[field, at], refs)
+        for refs in ((u_in, u_held, u_out), (v_in, v_held, v_out))
+        for field in range(2)
+        for at in (pl.ds(0, 64), pl.ds(64, 61))
+    ]
+    pieces += [
+        (lambda ref, at=at: ref.at[at], (k_in, k_held, k_out)) for at in (pl.ds(0, 64), pl.ds(64, 61))
+    ]
     inward = [
-        pltpu.make_async_copy(source, target, sems.at[i])
-        for i, (source, target) in enumerate(zip((u_in, v_in, k_in), held))
+        pltpu.make_async_copy(view(refs[0]), view(refs[1]), sems.at[0, i])
+        for i, (view, refs) in enumerate(pieces)
     ]
     outward = [
-        pltpu.make_async_copy(source, target, sems.at[3 + i])
-        for i, (source, target) in enumerate(zip(held, (u_out, v_out, k_out)))
+        pltpu.make_async_copy(view(refs[1]), view(refs[2]), sems.at[1, i])
+        for i, (view, refs) in enumerate(pieces)
     ]
     for copy in inward:
         copy.start()
@@ -647,7 +671,7 @@
             pltpu.VMEM((STEPS, 2, 25, 4, 128), f32),
             pltpu.VMEM((STEPS, 2, 25, 4, 128), f32),
             dma((8,)),
-            dma((3,)),
+            dma((13,)),
             dma((cuts,)),
             dma((cuts,)),
             dma((cuts,)),
@@ -668,7 +692,7 @@
         out_shape=shapes,
         in_specs=[hbm] * 3,
         out_specs=(hbm, hbm, hbm),
-        scratch_shapes=[pltpu.VMEM(x.shape, x.dtype) for x in shapes] + [dma((6,))],
+        scratch_shapes=[pltpu.VMEM(x.shape, x.dtype) for x in shapes] + [dma((2, 10))],
         compiler_params=pltpu.CompilerParams(vmem_limit_bytes=63 * 1024 * 1024),
     )(*out)
     return (

time: 31.8 us -> 31.7 us (level)
  no operation moved by 1% of the time
where the time goes in v2:
time: 31.7 us; the launch traced here: 31.5 us
  Pallas kernels  30.9 us (97%)
  between operations  0.64 us (2%)
    pallas_call x1, Pallas kernels, body(): pl.pallas_call(functools.partial(body_kernel, cuts, room), out_shape=shap...  29 us
    pallas_call x1, Pallas kernels, body(): pl.pallas_call(store_kernel, out_shape=shapes, in_specs=[hbm] * 3, out_sp...  1.91 us

profile of v2, /device:TPU:7, one launch (start us, length us, event | category | flops | bytes accessed | tf_op | source)
XLA Modules:
  0.0 31.5 jit_solution(2775860142329196343)
XLA Ops:
  0.6 29.0 %shard_map.103 = (f32[2,125,2,128]{3,2,1,0:T(2,128)}, f32[2,125,2,128]{3,2,1,0:T(2,128)}, f32[125,2,128]{2,1,0:T(2,128)}) custom-call(f32[2,125,2,128]{3,2,1,0:T(2,128)} %bitcast.11, f32[2,125,2,128]{3,2,1,0:T(2,128)} %bitcast.12, f32[2,128]{1,0:T(2,128)} %bitcast.15, f32[2,128]{1,0:T(2,128)} %bitcast.16, f32[125,2,128]{2,1,0:T(2,128)} %bitcast.14, ...), custom_call_target="tpu_custom_call" | custom-call | tf_op jit(solution)/shard_map/pallas_call | solution.py:649
  29.6 1.9 %shard_map.104 = (f32[2,125,2,128]{3,2,1,0:T(2,128)}, f32[2,125,2,128]{3,2,1,0:T(2,128)}, f32[125,2,128]{2,1,0:T(2,128)}) custom-call(f32[2,125,2,128]{3,2,1,0:T(2,128)} %get-tuple-element.9.u_in, f32[2,125,2,128]{3,2,1,0:T(2,128)} %get-tuple-element.10.v_in, f32[125,2,128]{2,1,0:T(2,128)} %get-tuple-element.11.k_in), custom_call_target="tpu_custom_call" | custom-call | tf_op jit(solution)/shard_map/pallas_call | solution.py:690
